TPU v7x, 32 devices: a whole 2x2x4 slice. The times are simulated.
32 devices in a mesh: groups: 2 (over x), expert: 8 (over z, y), tensor: 2 (over core).
Axes of the slice: x: 2, y: 2, z: 4, core: 2. Of those that a mesh axis runs over, the one named last changes fastest.
Arguments:
- quant_rows: bfloat16 [512, 3072], P(('groups', 'expert', 'tensor')), parts along dimension 0, may hold values from -6 to 6
- block_exps: int32 [512, 24], P(('groups', 'expert', 'tensor')), parts along dimension 0, may hold values from -2 to 1
- expert_ids: int32 [512, 4], P(('groups', 'expert', 'tensor')), parts along dimension 0, may hold values from 0 to 7, all different within a row; in each aligned block of 16 rows (0 to 15, 16 to 31, ...) at most 8 rows name the same one
- route_weights: float32 [512, 4], P(('groups', 'expert', 'tensor')), parts along dimension 0, may hold values from 0.1 to 1
- gate_weight: bfloat16 [8, 3072, 5376], P('expert', None, 'tensor'), may hold values from -0.109375 to 0.109375
- up_weight: bfloat16 [8, 3072, 5376], P('expert', None, 'tensor'), may hold values from -0.109375 to 0.109375
- down_weight: bfloat16 [8, 5376, 3072], P('expert', 'tensor'), may hold values from -0.078125 to 0.078125
- cotangent: bfloat16 [512, 3072], P(('groups', 'expert', 'tensor')), parts along dimension 0, may hold values from -6 to 6
Outputs:
- mixed: bfloat16 [512, 3072], P(('groups', 'expert', 'tensor')), parts along dimension 0
- grad_tokens: bfloat16 [512, 3072], P(('groups', 'expert', 'tensor')), parts along dimension 0
- grad_weights: float32 [512, 4], P(('groups', 'expert', 'tensor')), parts along dimension 0
There are 2 independent parts, one for each index of `groups`. A program takes and returns all parts, laid end to end along the dimension named above; an argument that names none is the same for every part. Nothing has to cross between parts.
Inputs may be any that keep to these rules, and one draw needn't show every extreme that they name: `expert_ids`: each token names 4 different experts. In each aligned block of 16 tokens (the tokens of one device) no expert is named by more than 8 tokens, a bound that some block reaches.
All inputs are finite; a program needn't handle non-finite values.
Results may differ from a plain program's by a relative error of at most 0.0064.
Values may be sent and summed in bfloat16 or wider, within the bound.
A program may use at most 128 MiB of HBM per device.

v0:
```python
import jax
import jax.numpy as jnp
from jax import lax
from jax.sharding import PartitionSpec as P

CAP = 8


def expert_pass(rows, grads, gate_w, up_w, down_w):
    gate = jnp.dot(rows, gate_w, preferred_element_type=jnp.float32)
    up = jnp.dot(rows, up_w, preferred_element_type=jnp.float32)
    sig = jax.nn.sigmoid(gate)
    act = gate * sig
    hidden = (act * up).astype(jnp.bfloat16)
    out_part = jnp.dot(hidden, down_w, preferred_element_type=jnp.float32)
    back = lax.dot_general(
        grads, down_w, (((1,), (1,)), ((), ())), preferred_element_type=jnp.float32
    )
    d_gate = (back * up * sig * (1.0 + gate * (1.0 - sig))).astype(jnp.bfloat16)
    d_up = (back * act).astype(jnp.bfloat16)
    in_part = lax.dot_general(
        d_gate, gate_w, (((1,), (1,)), ((), ())), preferred_element_type=jnp.float32
    )
    in_part = in_part + lax.dot_general(
        d_up, up_w, (((1,), (1,)), ((), ())), preferred_element_type=jnp.float32
    )
    return (out_part, in_part)


def body(
    quant_rows,
    block_exps,
    expert_ids,
    route_weights,
    gate_weight,
    up_weight,
    down_weight,
    cotangent,
):
    tok_rows, width = quant_rows.shape
    blocks = block_exps.shape[1]
    picks = expert_ids.shape[1]
    experts = lax.axis_size("expert")
    pair = lax.axis_size("tensor")
    scales = jnp.exp2(block_exps.astype(jnp.float32))
    tokens = (
        (
            quant_rows.astype(jnp.float32).reshape(tok_rows, blocks, width // blocks)
            * scales[:, :, None]
        )
        .reshape(tok_rows, width)
        .astype(jnp.bfloat16)
    )
    flat_ids = expert_ids.reshape(-1)
    onehot = (flat_ids[:, None] == jnp.arange(experts, dtype=jnp.int32)[None, :]).astype(jnp.int32)
    before = jnp.cumsum(onehot, axis=0) - onehot
    slot = jnp.sum(before * onehot, axis=1)
    target = flat_ids * CAP + slot
    placer = (jnp.arange(experts * CAP, dtype=jnp.int32)[:, None] == target[None, :]).astype(
        jnp.bfloat16
    )
    placer_tok = jnp.sum(
        placer.reshape(experts * CAP, tok_rows, picks).astype(jnp.float32), axis=2
    ).astype(jnp.bfloat16)
    grad32 = cotangent.astype(jnp.float32)
    scaled_grad = (
        (route_weights[:, :, None] * grad32[:, None, :])
        .astype(jnp.bfloat16)
        .reshape(tok_rows * picks, width)
    )
    send_x = (
        jnp.dot(placer_tok, tokens, preferred_element_type=jnp.float32)
        .astype(jnp.bfloat16)
        .reshape(experts, CAP, width)
    )
    send_g = (
        jnp.dot(placer, scaled_grad, preferred_element_type=jnp.float32)
        .astype(jnp.bfloat16)
        .reshape(experts, CAP, width)
    )
    gate_w = gate_weight[0]
    up_w = up_weight[0]
    down_w = down_weight[0]
    dup_x = jnp.broadcast_to(send_x[:, None], (experts, pair, CAP, width)).reshape(
        experts * pair, CAP, width
    )
    dup_g = jnp.broadcast_to(send_g[:, None], (experts, pair, CAP, width)).reshape(
        experts * pair, CAP, width
    )
    got_x, got_g = (
        lax.all_to_all(dup_x, ("expert", "tensor"), split_axis=0, concat_axis=0, tiled=True),
        lax.all_to_all(dup_g, ("expert", "tensor"), split_axis=0, concat_axis=0, tiled=True),
    )
    out_part, in_part = expert_pass(
        got_x.reshape(-1, width), got_g.reshape(-1, width), gate_w, up_w, down_w
    )
    back_y, back_dx = (
        lax.all_to_all(
            out_part.reshape(experts * pair, CAP, width),
            ("expert", "tensor"),
            split_axis=0,
            concat_axis=0,
            tiled=True,
        ),
        lax.all_to_all(
            in_part.reshape(experts * pair, CAP, width),
            ("expert", "tensor"),
            split_axis=0,
            concat_axis=0,
            tiled=True,
        ),
    )
    y_back = (
        jnp.sum(back_y.reshape(experts, pair, CAP, width), axis=1)
        .astype(jnp.bfloat16)
        .reshape(experts * CAP, width)
    )
    dx_back = (
        jnp.sum(back_dx.reshape(experts, pair, CAP, width), axis=1)
        .astype(jnp.bfloat16)
        .reshape(experts * CAP, width)
    )
    picked_y = lax.dot_general(
        placer, y_back, (((0,), (0,)), ((), ())), preferred_element_type=jnp.float32
    ).reshape(tok_rows, picks, width)
    picked_dx = lax.dot_general(
        placer, dx_back, (((0,), (0,)), ((), ())), preferred_element_type=jnp.float32
    ).reshape(tok_rows, picks, width)
    mixed = jnp.sum(route_weights[:, :, None] * picked_y, axis=1).astype(jnp.bfloat16)
    grad_tokens = jnp.sum(picked_dx, axis=1).astype(jnp.bfloat16)
    grad_weights = jnp.sum(grad32[:, None, :] * picked_y, axis=2)
    return (mixed, grad_tokens, grad_weights)


def solution(mesh):
    in_specs = (
        P(("groups", "expert", "tensor"), None),
        P(("groups", "expert", "tensor"), None),
        P(("groups", "expert", "tensor"), None),
        P(("groups", "expert", "tensor"), None),
        P("expert", None, "tensor"),
        P("expert", None, "tensor"),
        P("expert", "tensor", None),
        P(("groups", "expert", "tensor"), None),
    )
    out_specs = (
        P(("groups", "expert", "tensor"), None),
        P(("groups", "expert", "tensor"), None),
        P(("groups", "expert", "tensor"), None),
    )
    return jax.shard_map(body, mesh=mesh, in_specs=in_specs, out_specs=out_specs, check_vma=False)
```

profile of v0, /device:TPU:13, one launch (start us, length us, event | category | flops | bytes accessed | tf_op | source)
XLA Modules:
  0.0 182.7 jit_solution(6711124646742122534)
XLA Ops:
  0.6 0.8 copy.27
  1.4 0.1 reshape.120
  1.6 0.1 reduce_window_sum.11
  1.7 0.2 select_reduce_fusion
  1.9 1.1 mul.96.clone
  2.9 0.3 mul.97
  3.2 0.1 copy.30
  3.3 0.1 mul.94
  3.4 0.3 fusion.19
  3.8 1.0 broadcast_in_dim.11
  4.7 6.6 %all-to-all-start.2 = ((bf16[16,8,3072]{2,1,0:T(8,128)(2,1)}), bf16[16,8,3072]{2,1,0:T(8,128)(2,1)S(1)}, u32[]{:S(2)}, u32[]{:S(2)}) async-start(bf16[16,8,3072]{2,1,0:T(8,128)(2,1)} %bitcast.13), calls=%async_computation.2 | async-start | bytes 1572864 | tf_op jit(solution)/shard_map/all_to_all | solution.py:92
  11.3 0.1 reduce_sum.69
  11.4 0.1 copy.28
  11.4 0.1 fusion.41
  11.6 0.1 mul.88
  11.7 0.3 fusion.18
  12.0 18.5 %all-to-all-done.2 = bf16[16,8,3072]{2,1,0:T(8,128)(2,1)S(1)} async-done(((bf16[16,8,3072]{2,1,0:T(8,128)(2,1)}), bf16[16,8,3072]{2,1,0:T(8,128)(2,1)S(1)}, u32[]{:S(2)}, u32[]{:S(2)}) %all-to-all-start.2) | async-done | bytes 786464 | tf_op jit(solution)/shard_map/all_to_all | solution.py:92
  30.5 1.0 broadcast_in_dim.9
  31.5 5.0 %all-to-all-start = ((bf16[16,8,3072]{2,1,0:T(8,128)(2,1)}), bf16[16,8,3072]{2,1,0:T(8,128)(2,1)S(1)}, u32[]{:S(2)}, u32[]{:S(2)}) async-start(bf16[16,8,3072]{2,1,0:T(8,128)(2,1)} %bitcast.2), calls=%async_computation | async-start | bytes 1572864 | tf_op jit(solution)/shard_map/all_to_all | solution.py:91
  36.4 12.2 %fusion.2 = f32[128,2688]{1,0:T(8,128)} fusion(bf16[1,2688,3072]{2,1,0:T(8,128)(2,1)} %param.14, bf16[16,8,3072]{2,1,0:T(8,128)(2,1)S(1)} %all-to-all-done.2), kind=kOutput, calls=%fused_computation.2 | convolution fusion | flops 2113929216 | bytes 18677760 | tf_op jit(solution)/shard_map/dot_general | solution.py:16
  48.6 7.0 %all-to-all-done = bf16[16,8,3072]{2,1,0:T(8,128)(2,1)S(1)} async-done(((bf16[16,8,3072]{2,1,0:T(8,128)(2,1)}), bf16[16,8,3072]{2,1,0:T(8,128)(2,1)S(1)}, u32[]{:S(2)}, u32[]{:S(2)}) %all-to-all-start) | async-done | bytes 786464 | tf_op jit(solution)/shard_map/all_to_all | solution.py:91
  55.7 8.1 %fusion.10 = f32[128,2688]{1,0:T(8,128)S(1)} fusion(bf16[1,3072,2688]{2,1,0:T(8,128)(2,1)} %param.12, bf16[16,8,3072]{2,1,0:T(8,128)(2,1)S(1)} %all-to-all-done), kind=kOutput, calls=%fused_computation.10 | convolution fusion | flops 2113929216 | bytes 18677760 | tf_op jit(solution)/shard_map/dot_general | solution.py:10
  63.8 12.7 %fusion.4 = f32[128,3072]{1,0:T(8,128)} fusion(bf16[1,3072,2688]{2,1,0:T(8,128)(2,1)} %param.13, f32[128,2688]{1,0:T(8,128)} %fusion.2, f32[128,2688]{1,0:T(8,128)S(1)} %fusion.10), kind=kOutput, calls=%fused_computation.4 | convolution fusion | flops 2115993600 | bytes 20840448 | tf_op jit(solution)/shard_map/dot_general | solution.py:24
  76.5 9.2 %fusion.6 = f32[128,2688]{1,0:T(8,128)} fusion(bf16[1,3072,2688]{2,1,0:T(8,128)(2,1)} %param.13, bf16[16,8,3072]{2,1,0:T(8,128)(2,1)S(1)} %all-to-all-done), kind=kOutput, calls=%fused_computation.6 | convolution fusion | flops 2113929216 | bytes 18677760 | tf_op jit(solution)/shard_map/dot_general | solution.py:11
  85.7 13.7 %fusion.15 = f32[16,8,3072]{2,1,0:T(8,128)} fusion(f32[128,3072]{1,0:T(8,128)} %fusion.4, bf16[1,3072,2688]{2,1,0:T(8,128)(2,1)} %param.12, f32[128,2688]{1,0:T(8,128)S(1)} %fusion.10, f32[128,2688]{1,0:T(8,128)} %fusion.2, f32[128,2688]{1,0:T(8,128)} %fusion.6), kind=kOutput, calls=%fused_computation.13 | convolution fusion | flops 2117763072 | bytes 23789568 | tf_op jit(solution)/shard_map/dot_general | solution.py:21
  99.4 5.0 %all-to-all-start.3 = ((f32[16,8,3072]{2,1,0:T(8,128)}), f32[16,8,3072]{2,1,0:T(8,128)S(1)}, u32[]{:S(2)}, u32[]{:S(2)}) async-start(f32[16,8,3072]{2,1,0:T(8,128)} %fusion.15), calls=%async_computation.3 | async-start | bytes 3145728 | tf_op jit(solution)/shard_map/all_to_all | solution.py:105
  104.3 9.7 %fusion = f32[16,8,3072]{2,1,0:T(8,128)} fusion(bf16[1,2688,3072]{2,1,0:T(8,128)(2,1)} %param.14, f32[128,2688]{1,0:T(8,128)} %fusion.6, f32[128,2688]{1,0:T(8,128)S(1)} %fusion.10), kind=kOutput, calls=%fused_computation | convolution fusion | flops 2115993600 | bytes 20840448 | tf_op jit(solution)/shard_map/dot_general | solution.py:15
  114.1 26.4 %all-to-all-done.3 = f32[16,8,3072]{2,1,0:T(8,128)S(1)} async-done(((f32[16,8,3072]{2,1,0:T(8,128)}), f32[16,8,3072]{2,1,0:T(8,128)S(1)}, u32[]{:S(2)}, u32[]{:S(2)}) %all-to-all-start.3) | async-done | bytes 1572896 | tf_op jit(solution)/shard_map/all_to_all | solution.py:105
  140.5 4.9 %all-to-all-start.1 = ((f32[16,8,3072]{2,1,0:T(8,128)}), f32[16,8,3072]{2,1,0:T(8,128)S(1)}, u32[]{:S(2)}, u32[]{:S(2)}) async-start(f32[16,8,3072]{2,1,0:T(8,128)} %fusion), calls=%async_computation.1 | async-start | bytes 3145728 | tf_op jit(solution)/shard_map/all_to_all | solution.py:98
  145.6 0.9 convolution_reduce_fusion
  146.5 35.1 %all-to-all-done.1 = f32[16,8,3072]{2,1,0:T(8,128)S(1)} async-done(((f32[16,8,3072]{2,1,0:T(8,128)}), f32[16,8,3072]{2,1,0:T(8,128)S(1)}, u32[]{:S(2)}, u32[]{:S(2)}) %all-to-all-start.1) | async-done | bytes 1572896 | tf_op jit(solution)/shard_map/all_to_all | solution.py:98
  181.7 1.0 multiply_reduce_fusion
  (18 shorter events, 0.4 us)
Async XLA Ops:
  0.6 2.6 %copy-start.4 = (f32[16,4]{0,1:T(4,128)S(1)}, f32[16,4]{0,1:T(4,128)}, u32[]{:S(2)}) copy-start(f32[16,4]{0,1:T(4,128)} %param.11) | copy-start | bytes 772
  3.7 7.7 %copy-start.2 = (s32[16,4]{0,1:T(4,128)S(1)}, s32[16,4]{0,1:T(4,128)}, u32[]{:S(2)}) copy-start(s32[16,4]{0,1:T(4,128)} %param.10) | copy-start | bytes 772
  3.7 7.8 %copy-start.3 = (s32[16,24]{1,0:T(8,128)S(1)}, s32[16,24]{1,0:T(8,128)}, u32[]{:S(2)}) copy-start(s32[16,24]{1,0:T(8,128)} %param.9) | copy-start | bytes 4612
  3.7 7.9 %copy-start.1 = (bf16[16,3072]{1,0:T(8,128)(2,1)S(1)}, bf16[16,3072]{1,0:T(8,128)(2,1)}, u32[]{:S(2)}) copy-start(bf16[16,3072]{1,0:T(8,128)(2,1)} %param.8) | copy-start | bytes 294916
  4.7 25.8 %all-to-all-start.2 = ((bf16[16,8,3072]{2,1,0:T(8,128)(2,1)}), bf16[16,8,3072]{2,1,0:T(8,128)(2,1)S(1)}, u32[]{:S(2)}, u32[]{:S(2)}) async-start(bf16[16,8,3072]{2,1,0:T(8,128)(2,1)} %bitcast.13), calls=%async_computation.2 | async-start | bytes 1572864 | tf_op jit(solution)/shard_map/all_to_all | solution.py:92
  31.5 24.2 %all-to-all-start = ((bf16[16,8,3072]{2,1,0:T(8,128)(2,1)}), bf16[16,8,3072]{2,1,0:T(8,128)(2,1)S(1)}, u32[]{:S(2)}, u32[]{:S(2)}) async-start(bf16[16,8,3072]{2,1,0:T(8,128)(2,1)} %bitcast.2), calls=%async_computation | async-start | bytes 1572864 | tf_op jit(solution)/shard_map/all_to_all | solution.py:91
  99.4 41.1 %all-to-all-start.3 = ((f32[16,8,3072]{2,1,0:T(8,128)}), f32[16,8,3072]{2,1,0:T(8,128)S(1)}, u32[]{:S(2)}, u32[]{:S(2)}) async-start(f32[16,8,3072]{2,1,0:T(8,128)} %fusion.15), calls=%async_computation.3 | async-start | bytes 3145728 | tf_op jit(solution)/shard_map/all_to_all | solution.py:105
  114.1 31.4 %copy-start = (bf16[16,3072]{1,0:T(8,128)(2,1)S(1)}, bf16[16,3072]{1,0:T(8,128)(2,1)}, u32[]{:S(2)}) copy-start(bf16[16,3072]{1,0:T(8,128)(2,1)} %param.15) | copy-start | bytes 294916
  140.5 41.1 %all-to-all-start.1 = ((f32[16,8,3072]{2,1,0:T(8,128)}), f32[16,8,3072]{2,1,0:T(8,128)S(1)}, u32[]{:S(2)}, u32[]{:S(2)}) async-start(f32[16,8,3072]{2,1,0:T(8,128)} %fusion), calls=%async_computation.1 | async-start | bytes 3145728 | tf_op jit(solution)/shard_map/all_to_all | solution.py:98
where the time goes:
time: 183 us
  waiting for transfers between devices  87.1 us (48%)
  matrix products  68.2 us (37%)
  starting transfers between devices  21.4 us (12%)
  local copies, waits for them, and re-layouts  4.55 us (2%)
    all_to_all x1, waiting for transfers between devices, body(): lax.all_to_all(out_part.reshape(experts * pair, CAP, width), ('expert', '...  35.1 us
    all_to_all x1, waiting for transfers between devices, body(): lax.all_to_all(in_part.reshape(experts * pair, CAP, width), ('expert', 't...  26.4 us
    all_to_all x1, waiting for transfers between devices, body(): lax.all_to_all(dup_g, ('expert', 'tensor'), split_axis=0, concat_axis=0,...  18.5 us
    dot_general x1, matrix products, expert_pass(): lax.dot_general(d_gate, gate_w, (((1,), (1,)), ((), ())), preferred_eleme...  13.7 us
    dot_general x1, matrix products, expert_pass(): lax.dot_general(d_up, up_w, (((1,), (1,)), ((), ())), preferred_element_t...  12.7 us
    dot_general x1, matrix products, expert_pass(): lax.dot_general(grads, down_w, (((1,), (1,)), ((), ())), preferred_elemen...  12.2 us
    dot_general x1, matrix products, expert_pass(): out_part = jnp.dot(hidden, down_w, preferred_element_type=jnp.float32)  9.74 us
    dot_general x1, matrix products, expert_pass(): up = jnp.dot(rows, up_w, preferred_element_type=jnp.float32)  9.21 us
  transfers between devices with their start and end apart: 4, of which 4 were waited for; matrix products, arithmetic and copies ran while one was open for 13% of the time, Pallas kernels for 0%

commit v1 on v0

--- a/solution.py
+++ b/solution.py
@@ -1,9 +1,258 @@
+import functools
+
 import jax
 import jax.numpy as jnp
 from jax import lax
+from jax.experimental import pallas as pl
+from jax.experimental.pallas import tpu as pltpu
 from jax.sharding import PartitionSpec as P
 
 CAP = 8
+
+MESH = pl.DeviceIdType.MESH
+NT = (((1,), (1,)), ((), ()))
+CHUNKS = 4
+F_TILES = 3
+D_TILES = 3
+E_TILES = 7
+
+
+def fused_kernel(
+    experts,
+    xg_hbm,
+    gate_hbm,
+    up_hbm,
+    down_hbm,
+    ret_hbm,
+    gw,
+    uw,
+    dw,
+    rx,
+    acc,
+    hid,
+    own,
+    pair_out,
+    pair_in,
+    back_out,
+    w_sem,
+    d_send,
+    d_recv,
+    f_send,
+    f_recv,
+    p_send,
+    p_recv,
+    r_send,
+    r_recv,
+):
+    chunks, dc, ff = gw.shape
+    half = experts * CAP
+    me = lax.axis_index("expert")
+    core = lax.axis_index("tensor")
+    mate = {"tensor": 1 - core}
+
+    def weight_copies(c):
+        cols = pl.ds(c * dc, dc)
+        return (
+            pltpu.make_async_copy(gate_hbm.at[cols, :], gw.at[c], w_sem.at[0, c]),
+            pltpu.make_async_copy(up_hbm.at[cols, :], uw.at[c], w_sem.at[1, c]),
+            pltpu.make_async_copy(down_hbm.at[:, cols], dw.at[c], w_sem.at[2, c]),
+        )
+
+    def own_copy(c):
+        return pltpu.make_async_copy(
+            xg_hbm.at[me, :, pl.ds(c * dc, dc)], rx.at[c, 0, 0], d_recv.at[c, 0]
+        )
+
+    def dispatch(c, j):
+        peer = lax.rem(me + j, experts)
+        return pltpu.make_async_remote_copy(
+            src_ref=xg_hbm.at[peer, :, pl.ds(c * dc, dc)],
+            dst_ref=rx.at[c, 0, j],
+            send_sem=d_send.at[c, j],
+            recv_sem=d_recv.at[c, j],
+            device_id={"expert": peer},
+            device_id_type=MESH,
+        )
+
+    def forward(c):
+        return pltpu.make_async_remote_copy(
+            src_ref=rx.at[c, 0],
+            dst_ref=rx.at[c, 1],
+            send_sem=f_send.at[c],
+            recv_sem=f_recv.at[c],
+            device_id=mate,
+            device_id_type=MESH,
+        )
+
+    def pair(c):
+        return pltpu.make_async_remote_copy(
+            src_ref=pair_out.at[c % 2],
+            dst_ref=pair_in.at[c],
+            send_sem=p_send.at[c],
+            recv_sem=p_recv.at[c],
+            device_id=mate,
+            device_id_type=MESH,
+        )
+
+    def own_back(c):
+        return pltpu.make_async_copy(
+            back_out.at[c, 0], ret_hbm.at[me, :, pl.ds(c * dc, dc)], r_recv.at[c, 0]
+        )
+
+    def give_back(c, j):
+        return pltpu.make_async_remote_copy(
+            src_ref=back_out.at[c, j],
+            dst_ref=ret_hbm.at[me, :, pl.ds(c * dc, dc)],
+            send_sem=r_send.at[c, j],
+            recv_sem=r_recv.at[c, j],
+            device_id={"expert": lax.rem(me + experts - j, experts)},
+            device_id_type=MESH,
+        )
+
+    for copy in weight_copies(0):
+        copy.start()
+
+    barrier = pltpu.get_barrier_semaphore()
+    for j in range(1, experts):
+        pl.semaphore_signal(
+            barrier,
+            inc=1,
+            device_id={"expert": lax.rem(me + j, experts)},
+            device_id_type=MESH,
+        )
+    pl.semaphore_signal(barrier, inc=1, device_id=mate, device_id_type=MESH)
+    pl.semaphore_wait(barrier, experts)
+
+    for c in range(chunks):
+        own_copy(c).start()
+        for j in range(1, experts):
+            dispatch(c, j).start()
+    for c in range(1, chunks):
+        for copy in weight_copies(c):
+            copy.start()
+
+    def collect(c):
+        own_copy(c).wait()
+        for j in range(1, experts):
+            dispatch(c, j).wait_recv()
+        forward(c).start()
+
+    f_tile = ff // F_TILES
+    collect(0)
+    for c in range(chunks):
+        if c + 1 < chunks:
+            collect(c + 1)
+        forward(c).wait_recv()
+        for copy in weight_copies(c):
+            copy.wait()
+        both = rx[c].astype(jnp.float32)
+        xs = both[:, :, :CAP, :].reshape(2 * half, dc).astype(jnp.bfloat16)
+        gs = both[:, :, CAP:, :].reshape(2 * half, dc).astype(jnp.bfloat16)
+        for f in range(F_TILES):
+            cols = pl.ds(f * f_tile, f_tile)
+            gate = jnp.dot(xs, gw[c, :, cols], preferred_element_type=jnp.float32)
+            up = jnp.dot(xs, uw[c, :, cols], preferred_element_type=jnp.float32)
+            back = lax.dot_general(gs, dw[c, cols, :], NT, preferred_element_type=jnp.float32)
+            if c == 0:
+                acc[0, :, cols] = gate
+                acc[1, :, cols] = up
+                acc[2, :, cols] = back
+            else:
+                acc[0, :, cols] += gate
+                acc[1, :, cols] += up
+                acc[2, :, cols] += back
+
+    e_tile = ff // E_TILES
+    for e in range(E_TILES):
+        cols = pl.ds(e * e_tile, e_tile)
+        gate = acc[0, :, cols]
+        up = acc[1, :, cols]
+        back = acc[2, :, cols]
+        sig = jax.nn.sigmoid(gate)
+        act = gate * sig
+        hid[0, :, cols] = (act * up).astype(jnp.bfloat16)
+        hid[1, :, cols] = (back * up * sig * (1.0 + gate * (1.0 - sig))).astype(jnp.bfloat16)
+        hid[2, :, cols] = (back * act).astype(jnp.bfloat16)
+
+    def finish(c):
+        pair(c).wait_recv()
+        tot = own[c % 2] + pair_in[c]
+        back_out[c] = tot.astype(jnp.bfloat16)
+        for j in range(1, experts):
+            give_back(c, j).start()
+        own_back(c).start()
+
+    d_tile = dc // D_TILES
+    for c in range(chunks):
+        if c >= 2:
+            pair(c - 2).wait_send()
+        for d in range(D_TILES):
+            cols = pl.ds(d * d_tile, d_tile)
+            y = jnp.dot(hid[0], dw[c, :, cols], preferred_element_type=jnp.float32)
+            dx = lax.dot_general(hid[1], gw[c, cols, :], NT, preferred_element_type=jnp.float32)
+            dx = dx + lax.dot_general(
+                hid[2], uw[c, cols, :], NT, preferred_element_type=jnp.float32
+            )
+            y = y.reshape(2, experts, CAP, d_tile)
+            dx = dx.reshape(2, experts, CAP, d_tile)
+            own[c % 2, :, :CAP, cols] = y[0]
+            own[c % 2, :, CAP:, cols] = dx[0]
+            pair_out[c % 2, :, :CAP, cols] = y[1]
+            pair_out[c % 2, :, CAP:, cols] = dx[1]
+        pair(c).start()
+        if c >= 1:
+            finish(c - 1)
+    finish(chunks - 1)
+
+    for c in range(chunks):
+        forward(c).wait_send()
+        if c >= chunks - 2:
+            pair(c).wait_send()
+        own_back(c).wait()
+        for j in range(1, experts):
+            dispatch(c, j).wait_send()
+            give_back(c, j).wait_send()
+            give_back(c, j).wait_recv()
+
+
+def fused_experts(xg, gate_w, up_w, down_w):
+    experts, _, width = xg.shape
+    ff = gate_w.shape[1]
+    c, dc, rows = CHUNKS, width // CHUNKS, 2 * experts * CAP
+    dma = pltpu.SemaphoreType.DMA
+    return pl.pallas_call(
+        functools.partial(fused_kernel, experts),
+        out_shape=jax.ShapeDtypeStruct(xg.shape, jnp.bfloat16),
+        in_specs=[pl.BlockSpec(memory_space=pl.ANY)] * 4,
+        out_specs=pl.BlockSpec(memory_space=pl.ANY),
+        scratch_shapes=[
+            pltpu.VMEM((c, dc, ff), jnp.bfloat16),
+            pltpu.VMEM((c, dc, ff), jnp.bfloat16),
+            pltpu.VMEM((c, ff, dc), jnp.bfloat16),
+            pltpu.VMEM((c, 2, experts, 2 * CAP, dc), jnp.bfloat16),
+            pltpu.VMEM((3, rows, ff), jnp.float32),
+            pltpu.VMEM((3, rows, ff), jnp.bfloat16),
+            pltpu.VMEM((2, experts, 2 * CAP, dc), jnp.float32),
+            pltpu.VMEM((2, experts, 2 * CAP, dc), jnp.float32),
+            pltpu.VMEM((c, experts, 2 * CAP, dc), jnp.float32),
+            pltpu.VMEM((c, experts, 2 * CAP, dc), jnp.bfloat16),
+            dma((3, c)),
+            dma((c, experts)),
+            dma((c, experts)),
+            dma((c,)),
+            dma((c,)),
+            dma((c,)),
+            dma((c,)),
+            dma((c, experts)),
+            dma((c, experts)),
+        ],
+        compiler_params=pltpu.CompilerParams(
+            collective_id=0, has_side_effects=True, vmem_limit_bytes=63 * 2**20
+        ),
+        cost_estimate=pl.CostEstimate(
+            flops=12 * rows * width * ff, bytes_accessed=6 * width * ff, transcendentals=rows * ff
+        ),
+    )(xg, gate_w, up_w, down_w)
 
 
 def expert_pass(rows, grads, gate_w, up_w, down_w):
@@ -25,6 +274,49 @@
         d_up, up_w, (((1,), (1,)), ((), ())), preferred_element_type=jnp.float32
     )
     return (out_part, in_part)
+
+
+def exchange(send_x, send_g, gate_w, up_w, down_w, experts, pair, width):
+    dup_x = jnp.broadcast_to(send_x[:, None], (experts, pair, CAP, width)).reshape(
+        experts * pair, CAP, width
+    )
+    dup_g = jnp.broadcast_to(send_g[:, None], (experts, pair, CAP, width)).reshape(
+        experts * pair, CAP, width
+    )
+    got_x, got_g = (
+        lax.all_to_all(dup_x, ("expert", "tensor"), split_axis=0, concat_axis=0, tiled=True),
+        lax.all_to_all(dup_g, ("expert", "tensor"), split_axis=0, concat_axis=0, tiled=True),
+    )
+    out_part, in_part = expert_pass(
+        got_x.reshape(-1, width), got_g.reshape(-1, width), gate_w, up_w, down_w
+    )
+    back_y, back_dx = (
+        lax.all_to_all(
+            out_part.reshape(experts * pair, CAP, width),
+            ("expert", "tensor"),
+            split_axis=0,
+            concat_axis=0,
+            tiled=True,
+        ),
+        lax.all_to_all(
+            in_part.reshape(experts * pair, CAP, width),
+            ("expert", "tensor"),
+            split_axis=0,
+            concat_axis=0,
+            tiled=True,
+        ),
+    )
+    y_back = (
+        jnp.sum(back_y.reshape(experts, pair, CAP, width), axis=1)
+        .astype(jnp.bfloat16)
+        .reshape(experts * CAP, width)
+    )
+    dx_back = (
+        jnp.sum(back_dx.reshape(experts, pair, CAP, width), axis=1)
+        .astype(jnp.bfloat16)
+        .reshape(experts * CAP, width)
+    )
+    return (y_back, dx_back)
 
 
 def body(
@@ -81,45 +373,12 @@
     gate_w = gate_weight[0]
     up_w = up_weight[0]
     down_w = down_weight[0]
-    dup_x = jnp.broadcast_to(send_x[:, None], (experts, pair, CAP, width)).reshape(
-        experts * pair, CAP, width
-    )
-    dup_g = jnp.broadcast_to(send_g[:, None], (experts, pair, CAP, width)).reshape(
-        experts * pair, CAP, width
-    )
-    got_x, got_g = (
-        lax.all_to_all(dup_x, ("expert", "tensor"), split_axis=0, concat_axis=0, tiled=True),
-        lax.all_to_all(dup_g, ("expert", "tensor"), split_axis=0, concat_axis=0, tiled=True),
-    )
-    out_part, in_part = expert_pass(
-        got_x.reshape(-1, width), got_g.reshape(-1, width), gate_w, up_w, down_w
-    )
-    back_y, back_dx = (
-        lax.all_to_all(
-            out_part.reshape(experts * pair, CAP, width),
-            ("expert", "tensor"),
-            split_axis=0,
-            concat_axis=0,
-            tiled=True,
-        ),
-        lax.all_to_all(
-            in_part.reshape(experts * pair, CAP, width),
-            ("expert", "tensor"),
-            split_axis=0,
-            concat_axis=0,
-            tiled=True,
-        ),
-    )
-    y_back = (
-        jnp.sum(back_y.reshape(experts, pair, CAP, width), axis=1)
-        .astype(jnp.bfloat16)
-        .reshape(experts * CAP, width)
-    )
-    dx_back = (
-        jnp.sum(back_dx.reshape(experts, pair, CAP, width), axis=1)
-        .astype(jnp.bfloat16)
-        .reshape(experts * CAP, width)
-    )
+    if experts <= 8:
+        ret = fused_experts(jnp.concatenate([send_x, send_g], axis=1), gate_w, up_w, down_w)
+        y_back = ret[:, :CAP].reshape(experts * CAP, width)
+        dx_back = ret[:, CAP:].reshape(experts * CAP, width)
+    else:
+        y_back, dx_back = exchange(send_x, send_g, gate_w, up_w, down_w, experts, pair, width)
     picked_y = lax.dot_general(
         placer, y_back, (((0,), (0,)), ((), ())), preferred_element_type=jnp.float32
     ).reshape(tok_rows, picks, width)

time: 183 us -> 72 us (0.39)
  the two profiles are of different devices: /device:TPU:13 before, /device:TPU:0 now
where the time goes in v1:
time: 72 us; the launch traced here: 71.6 us
  Pallas kernels  59.3 us (82%)
  matrix products  5.47 us (8%)
  local copies, waits for them, and re-layouts  3.3 us (5%)
  other arithmetic  2.86 us (4%)
  between operations  0.73 us (1%)
    pallas_call x1, Pallas kernels, fused_experts(): pl.pallas_call(functools.partial(fused_kernel, experts), out_shape=jax.Sh...  59.3 us
    dot_general x1, matrix products, body(): lax.dot_general(placer, y_back, (((0,), (0,)), ((), ())), preferred_eleme...  2.02 us
    dot_general x1, matrix products, body(): lax.dot_general(placer, dx_back, (((0,), (0,)), ((), ())), preferred_elem...  1.95 us
    unnamed x6, local copies, waits for them, and re-layouts  1.53 us

profile of v1, /device:TPU:0, one launch (start us, length us, event | category | flops | bytes accessed | tf_op | source)
XLA Modules:
  0.0 71.6 jit_solution(16606175992518791627)
XLA Ops:
  0.6 0.8 %copy.27 = s32[16,4]{1,0:T(8,128)S(1)} copy(s32[16,4]{0,1:T(4,128)} %param.10) | data formatting | bytes 512 | tf_op args[2]
  1.4 0.1 reshape.89
  1.5 0.1 fusion.10
  1.6 0.1 reduce_window_sum.11
  1.7 0.2 select_reduce_fusion
  1.8 1.1 %mul.72.clone = f32[16,4,3072]{2,1,0:T(4,128)S(1)} broadcast(bf16[16,3072]{1,0:T(8,128)(2,1)} %param.15), dimensions={0,2} | broadcast | bytes 884736 | tf_op jit(solution)/shard_map/mul | solution.py:359
  2.9 0.3 mul.73
  3.2 0.8 %copy.29 = f32[16,4]{1,0:T(8,128)S(1)} copy(f32[16,4]{0,1:T(4,128)} %param.11) | data formatting | bytes 512 | tf_op args[3]
  4.0 0.1 mul.70
  4.0 0.3 fusion.1
  4.4 0.1 reduce_sum.51
  4.5 0.1 copy.28
  4.5 0.7 multiply_add_fusion
  5.2 0.1 fusion.14
  5.3 0.7 multiply_exponential_fusion
  6.0 0.1 mul.67
  6.1 1.2 %fusion = bf16[8,8,3072]{2,1,0:T(8,128)(2,1)S(1)} fusion(bf16[64,16]{0,1:T(8,128)(2,1)S(1)} %fusion.14, f32[2,8,24,128]{3,2,1,0:T(8,128)S(1)} %bitcast.30, bf16[16,3072]{1,0:T(8,128)(2,1)} %param.8), kind=kOutput, calls=%fused_computation.2 | convolution fusion | flops 6635520 | bytes 690176 | tf_op jit(solution)/shard_map/dot_general | solution.py:364
  7.3 0.9 %pad_maximum_fusion.xg_hbm = bf16[8,16,3072]{2,1,0:T(8,128)(2,1)} fusion(bf16[8,8,3072]{2,1,0:T(8,128)(2,1)S(1)} %fusion.1, bf16[8,8,3072]{2,1,0:T(8,128)(2,1)S(1)} %fusion), kind=kLoop, calls=%fused_computation.5 | loop fusion | flops 1572864 | bytes 1572864 | tf_op jit(solution)/shard_map/concatenate | solution.py:377
  8.3 0.0 copy-start
  8.3 0.0 copy-start.1
  8.3 59.3 %shard_map.103 = bf16[8,16,3072]{2,1,0:T(8,128)(2,1)} custom-call(bf16[8,16,3072]{2,1,0:T(8,128)(2,1)} %pad_maximum_fusion.xg_hbm, bf16[3072,2688]{1,0:T(8,128)(2,1)} %bitcast.27, bf16[3072,2688]{1,0:T(8,128)(2,1)} %bitcast.28, bf16[2688,3072]{1,0:T(8,128)(2,1)} %bitcast.29), custom_call_target="tpu_custom_call" | custom-call | flops 12683575296 | bytes 49545216 | tf_op jit(solution)/shard_map/pallas_call | solution.py:223
  67.6 0.1 iota_compare_fusion.3
  67.6 0.0 copy-done
  67.7 0.0 copy-done.1
  67.7 2.0 %multiply_reduce_fusion = (f32[16,4]{0,1:T(4,128)}, bf16[16,3072]{1,0:T(8,128)(2,1)}) fusion(f32[16,3072]{1,0:T(8,128)S(1)} %convert_element_type.43, f32[16,4]{0,1:T(4,128)S(1)} %copy-done.1, bf16[8,16,3072]{2,1,0:T(8,128)(2,1)} %shard_map.103, pred[16,4,64]{2,1,0:T(4,128)(4,1)S(1)} %bitcast.31), kind=kOutput, calls=%fused_computation.6 | convolution fusion | flops 25903040 | bytes 692736 | tf_op jit(solution)/shard_map/dot_general | solution.py:382
  69.7 1.9 %convolution_reduce_fusion = bf16[16,3072]{1,0:T(8,128)(2,1)} fusion(bf16[8,16,3072]{2,1,0:T(8,128)(2,1)} %shard_map.103, pred[16,4,64]{2,1,0:T(4,128)(4,1)S(1)} %bitcast.32), kind=kOutput, calls=%fused_computation.4 | convolution fusion | flops 25313280 | bytes 495616 | tf_op jit(solution)/shard_map/dot_general | solution.py:385
  (2 shorter events, 0.0 us)
Async XLA Ops:
  8.3 59.4 %copy-start = (bf16[16,3072]{1,0:T(8,128)(2,1)S(1)}, bf16[16,3072]{1,0:T(8,128)(2,1)}, u32[]{:S(2)}) copy-start(bf16[16,3072]{1,0:T(8,128)(2,1)} %param.15) | copy-start | bytes 294916
  8.3 59.4 %copy-start.1 = (f32[16,4]{0,1:T(4,128)S(1)}, f32[16,4]{0,1:T(4,128)}, u32[]{:S(2)}) copy-start(f32[16,4]{0,1:T(4,128)} %param.11) | copy-start | bytes 772

commit v2 on v1

--- a/solution.py
+++ b/solution.py
@@ -11,19 +11,29 @@
 
 MESH = pl.DeviceIdType.MESH
 NT = (((1,), (1,)), ((), ()))
-CHUNKS = 4
+TN = (((0,), (0,)), ((), ()))
+BLOCK = 128
+CHUNKS = 6
 F_TILES = 3
-D_TILES = 3
+D_TILES = 2
 E_TILES = 7
 
 
 def fused_kernel(
     experts,
-    xg_hbm,
+    q_ref,
+    exp_ref,
+    ids_ref,
+    wts_ref,
+    cot_ref,
     gate_hbm,
     up_hbm,
     down_hbm,
-    ret_hbm,
+    mixed_ref,
+    gtok_ref,
+    gwts_ref,
+    xg,
+    ret,
     gw,
     uw,
     dw,
@@ -33,7 +43,6 @@
     own,
     pair_out,
     pair_in,
-    back_out,
     w_sem,
     d_send,
     d_recv,
@@ -51,7 +60,7 @@
     mate = {"tensor": 1 - core}
 
     def weight_copies(c):
-        cols = pl.ds(c * dc, dc)
+        cols = pl.ds(pl.multiple_of(c * dc, dc), dc)
         return (
             pltpu.make_async_copy(gate_hbm.at[cols, :], gw.at[c], w_sem.at[0, c]),
             pltpu.make_async_copy(up_hbm.at[cols, :], uw.at[c], w_sem.at[1, c]),
@@ -60,13 +69,13 @@
 
     def own_copy(c):
         return pltpu.make_async_copy(
-            xg_hbm.at[me, :, pl.ds(c * dc, dc)], rx.at[c, 0, 0], d_recv.at[c, 0]
+            xg.at[c, me], rx.at[c, 0, 0], d_recv.at[c, 0]
         )
 
     def dispatch(c, j):
         peer = lax.rem(me + j, experts)
         return pltpu.make_async_remote_copy(
-            src_ref=xg_hbm.at[peer, :, pl.ds(c * dc, dc)],
+            src_ref=xg.at[c, peer],
             dst_ref=rx.at[c, 0, j],
             send_sem=d_send.at[c, j],
             recv_sem=d_recv.at[c, j],
@@ -96,22 +105,59 @@
 
     def own_back(c):
         return pltpu.make_async_copy(
-            back_out.at[c, 0], ret_hbm.at[me, :, pl.ds(c * dc, dc)], r_recv.at[c, 0]
+            xg.at[c, 0], ret.at[c, me], r_recv.at[c, 0]
         )
 
     def give_back(c, j):
         return pltpu.make_async_remote_copy(
-            src_ref=back_out.at[c, j],
-            dst_ref=ret_hbm.at[me, :, pl.ds(c * dc, dc)],
+            src_ref=xg.at[c, j],
+            dst_ref=ret.at[c, me],
             send_sem=r_send.at[c, j],
             recv_sem=r_recv.at[c, j],
             device_id={"expert": lax.rem(me + experts - j, experts)},
             device_id_type=MESH,
         )
 
-    for copy in weight_copies(0):
-        copy.start()
-
+    for c in range(chunks):
+        for copy in weight_copies(c):
+            copy.start()
+
+    toks, picks = ids_ref.shape
+    ids = ids_ref[...]
+    wts = wts_ref[...]
+    place = lax.broadcasted_iota(jnp.int32, (toks, half), 1)
+    hits = [(ids[:, k : k + 1] == place // CAP).astype(jnp.float32) for k in range(picks)]
+    named = hits[0]
+    for k in range(1, picks):
+        named = named + hits[k]
+    later = lax.broadcasted_iota(jnp.int32, (toks, toks), 0)
+    earlier = lax.broadcasted_iota(jnp.int32, (toks, toks), 1)
+    below = (earlier < later).astype(jnp.bfloat16)
+    before = jnp.dot(below, named.astype(jnp.bfloat16), preferred_element_type=jnp.float32)
+    in_slot = (before == (place % CAP).astype(jnp.float32)).astype(jnp.float32)
+    placer = jnp.concatenate([hit * in_slot for hit in hits], axis=0).astype(jnp.bfloat16)
+    placer_tok = (named * in_slot).astype(jnp.bfloat16)
+    exps = exp_ref[...]
+    scales = jnp.where(
+        exps >= 0, jnp.where(exps == 1, 2.0, 1.0), jnp.where(exps == -1, 0.5, 0.25)
+    ).astype(jnp.float32)
+
+    def prepare(c):
+        parts = []
+        for b in range(c * dc // BLOCK, (c + 1) * dc // BLOCK):
+            part = q_ref[:, b * BLOCK : (b + 1) * BLOCK].astype(jnp.float32)
+            parts.append((part * scales[:, b : b + 1]).astype(jnp.bfloat16))
+        toks_c = jnp.concatenate(parts, axis=1)
+        grad32 = cot_ref[:, pl.ds(c * dc, dc)].astype(jnp.float32)
+        scaled = jnp.concatenate([wts[:, k : k + 1] * grad32 for k in range(picks)], axis=0)
+        xs = lax.dot_general(placer_tok, toks_c, TN, preferred_element_type=jnp.float32)
+        gs = lax.dot_general(
+            placer, scaled.astype(jnp.bfloat16), TN, preferred_element_type=jnp.float32
+        )
+        both = [xs.reshape(experts, CAP, dc), gs.reshape(experts, CAP, dc)]
+        xg[c] = jnp.concatenate(both, axis=1).astype(jnp.bfloat16)
+
+    prepare(0)
     barrier = pltpu.get_barrier_semaphore()
     for j in range(1, experts):
         pl.semaphore_signal(
@@ -124,13 +170,11 @@
     pl.semaphore_wait(barrier, experts)
 
     for c in range(chunks):
+        if c > 0:
+            prepare(c)
         own_copy(c).start()
         for j in range(1, experts):
             dispatch(c, j).start()
-    for c in range(1, chunks):
-        for copy in weight_copies(c):
-            copy.start()
-
     def collect(c):
         own_copy(c).wait()
         for j in range(1, experts):
@@ -138,10 +182,7 @@
         forward(c).start()
 
     f_tile = ff // F_TILES
-    collect(0)
-    for c in range(chunks):
-        if c + 1 < chunks:
-            collect(c + 1)
+    def project(c):
         forward(c).wait_recv()
         for copy in weight_copies(c):
             copy.wait()
@@ -153,14 +194,20 @@
             gate = jnp.dot(xs, gw[c, :, cols], preferred_element_type=jnp.float32)
             up = jnp.dot(xs, uw[c, :, cols], preferred_element_type=jnp.float32)
             back = lax.dot_general(gs, dw[c, cols, :], NT, preferred_element_type=jnp.float32)
-            if c == 0:
-                acc[0, :, cols] = gate
-                acc[1, :, cols] = up
-                acc[2, :, cols] = back
-            else:
-                acc[0, :, cols] += gate
-                acc[1, :, cols] += up
-                acc[2, :, cols] += back
+            acc[0, :, cols] += gate
+            acc[1, :, cols] += up
+            acc[2, :, cols] += back
+
+    acc[...] = jnp.zeros_like(acc)
+    collect(0)
+
+    @pl.loop(0, chunks)
+    def _(c):
+        @pl.when(c + 1 < chunks)
+        def _():
+            collect(c + 1)
+
+        project(c)
 
     e_tile = ff // E_TILES
     for e in range(E_TILES):
@@ -174,10 +221,14 @@
         hid[1, :, cols] = (back * up * sig * (1.0 + gate * (1.0 - sig))).astype(jnp.bfloat16)
         hid[2, :, cols] = (back * act).astype(jnp.bfloat16)
 
+    for c in range(chunks):
+        for j in range(1, experts):
+            dispatch(c, j).wait_send()
+
     def finish(c):
         pair(c).wait_recv()
         tot = own[c % 2] + pair_in[c]
-        back_out[c] = tot.astype(jnp.bfloat16)
+        xg[c] = tot.astype(jnp.bfloat16)
         for j in range(1, experts):
             give_back(c, j).start()
         own_back(c).start()
@@ -204,28 +255,58 @@
             finish(c - 1)
     finish(chunks - 1)
 
+    lane = lax.broadcasted_iota(jnp.int32, (toks, picks), 1)
+    gwts_ref[...] = jnp.zeros_like(gwts_ref)
+
+    @pl.loop(0, chunks)
+    def _(c):
+        cols = pl.ds(pl.multiple_of(c * dc, dc), dc)
+        own_back(c).wait()
+        for j in range(1, experts):
+            give_back(c, j).wait_recv()
+        both = ret[c].astype(jnp.float32)
+        ys = both[:, :CAP, :].reshape(half, dc).astype(jnp.bfloat16)
+        dxs = both[:, CAP:, :].reshape(half, dc).astype(jnp.bfloat16)
+        picked = jnp.dot(placer, ys, preferred_element_type=jnp.float32)
+        grad32 = cot_ref[:, cols].astype(jnp.float32)
+        total = jnp.zeros((toks, dc), jnp.float32)
+        dots = jnp.zeros((toks, picks), jnp.float32)
+        for k in range(picks):
+            pick = picked[k * toks : (k + 1) * toks]
+            total = total + wts[:, k : k + 1] * pick
+            dots = jnp.where(lane == k, jnp.sum(grad32 * pick, axis=1, keepdims=True), dots)
+        gwts_ref[...] += dots
+        mixed_ref[:, cols] = total.astype(jnp.bfloat16)
+        gtok_ref[:, cols] = jnp.dot(
+            placer_tok, dxs, preferred_element_type=jnp.float32
+        ).astype(jnp.bfloat16)
+
     for c in range(chunks):
         forward(c).wait_send()
         if c >= chunks - 2:
             pair(c).wait_send()
-        own_back(c).wait()
-        for j in range(1, experts):
-            dispatch(c, j).wait_send()
+        for j in range(1, experts):
             give_back(c, j).wait_send()
-            give_back(c, j).wait_recv()
-
-
-def fused_experts(xg, gate_w, up_w, down_w):
-    experts, _, width = xg.shape
+
+
+def fused_experts(experts, rows_in, exps, ids, wts, cot, gate_w, up_w, down_w):
+    toks, width = rows_in.shape
     ff = gate_w.shape[1]
     c, dc, rows = CHUNKS, width // CHUNKS, 2 * experts * CAP
     dma = pltpu.SemaphoreType.DMA
     return pl.pallas_call(
         functools.partial(fused_kernel, experts),
-        out_shape=jax.ShapeDtypeStruct(xg.shape, jnp.bfloat16),
-        in_specs=[pl.BlockSpec(memory_space=pl.ANY)] * 4,
-        out_specs=pl.BlockSpec(memory_space=pl.ANY),
+        out_shape=(
+            jax.ShapeDtypeStruct((toks, width), jnp.bfloat16),
+            jax.ShapeDtypeStruct((toks, width), jnp.bfloat16),
+            jax.ShapeDtypeStruct(ids.shape, jnp.float32),
+        ),
+        in_specs=[pl.BlockSpec(memory_space=pltpu.VMEM)] * 5
+        + [pl.BlockSpec(memory_space=pl.ANY)] * 3,
+        out_specs=[pl.BlockSpec(memory_space=pltpu.VMEM)] * 3,
         scratch_shapes=[
+            pltpu.VMEM((c, experts, 2 * CAP, dc), jnp.bfloat16),
+            pltpu.VMEM((c, experts, 2 * CAP, dc), jnp.bfloat16),
             pltpu.VMEM((c, dc, ff), jnp.bfloat16),
             pltpu.VMEM((c, dc, ff), jnp.bfloat16),
             pltpu.VMEM((c, ff, dc), jnp.bfloat16),
@@ -235,7 +316,6 @@
             pltpu.VMEM((2, experts, 2 * CAP, dc), jnp.float32),
             pltpu.VMEM((2, experts, 2 * CAP, dc), jnp.float32),
             pltpu.VMEM((c, experts, 2 * CAP, dc), jnp.float32),
-            pltpu.VMEM((c, experts, 2 * CAP, dc), jnp.bfloat16),
             dma((3, c)),
             dma((c, experts)),
             dma((c, experts)),
@@ -252,7 +332,7 @@
         cost_estimate=pl.CostEstimate(
             flops=12 * rows * width * ff, bytes_accessed=6 * width * ff, transcendentals=rows * ff
         ),
-    )(xg, gate_w, up_w, down_w)
+    )(rows_in, exps, ids, wts, cot, gate_w, up_w, down_w)
 
 
 def expert_pass(rows, grads, gate_w, up_w, down_w):
@@ -334,6 +414,18 @@
     picks = expert_ids.shape[1]
     experts = lax.axis_size("expert")
     pair = lax.axis_size("tensor")
+    if experts <= 8:
+        return fused_experts(
+            experts,
+            quant_rows,
+            block_exps,
+            expert_ids,
+            route_weights,
+            cotangent,
+            gate_weight[0],
+            up_weight[0],
+            down_weight[0],
+        )
     scales = jnp.exp2(block_exps.astype(jnp.float32))
     tokens = (
         (
@@ -373,12 +465,7 @@
     gate_w = gate_weight[0]
     up_w = up_weight[0]
     down_w = down_weight[0]
-    if experts <= 8:
-        ret = fused_experts(jnp.concatenate([send_x, send_g], axis=1), gate_w, up_w, down_w)
-        y_back = ret[:, :CAP].reshape(experts * CAP, width)
-        dx_back = ret[:, CAP:].reshape(experts * CAP, width)
-    else:
-        y_back, dx_back = exchange(send_x, send_g, gate_w, up_w, down_w, experts, pair, width)
+    y_back, dx_back = exchange(send_x, send_g, gate_w, up_w, down_w, experts, pair, width)
     picked_y = lax.dot_general(
         placer, y_back, (((0,), (0,)), ((), ())), preferred_element_type=jnp.float32
     ).reshape(tok_rows, picks, width)

time: 72 us -> 67.1 us (0.932)
  matrix products: 5.47 us -> 0 us
  local copies, waits for them, and re-layouts: 3.3 us -> 7.14 us
  other arithmetic: 2.86 us -> 0 us
    dot_general x4 -> x0, matrix products: 5.47 us -> none  [the longest x1 2.02 us: body(): lax.dot_general(placer, y_back, (((0,), (0,)), ((), ())), preferred_eleme...]
    unnamed x6 -> x4, local copies, waits for them, and re-layouts: 1.53 us -> 5.79 us
    mul x4 -> x0, local copies, waits for them, and re-layouts: 1.52 us -> none  [the longest x2 1.33 us: body(): route_weights[:, :, None] * grad32[:, None, :]]
    pallas_call x0 -> x1, local copies, waits for them, and re-layouts: none -> 1.35 us  [fused_experts(): pl.pallas_call(functools.partial(fused_kernel, experts), out_shape=(jax.S...]
    concatenate x1 -> x0, other arithmetic: 0.93 us -> none  [body(): jnp.concatenate([send_x, send_g], axis=1)]
where the time goes in v2:
time: 67.1 us; the launch traced here: 66.8 us
  Pallas kernels  59 us (88%)
  local copies, waits for them, and re-layouts  7.14 us (11%)
    pallas_call x1, Pallas kernels, fused_experts(): pl.pallas_call(functools.partial(fused_kernel, experts), out_shape=(jax.S...  59 us
    unnamed x4, local copies, waits for them, and re-layouts  5.79 us
    pallas_call x1, local copies, waits for them, and re-layouts, fused_experts(): pl.pallas_call(functools.partial(fused_kernel, experts), out_shape=(jax.S...  1.35 us

profile of v2, /device:TPU:0, one launch (start us, length us, event | category | flops | bytes accessed | tf_op | source)
XLA Modules:
  0.0 66.8 jit_solution(1382533829461917150)
XLA Ops:
  0.6 1.4 %copy.11.ids_ref = s32[16,4]{1,0:T(8,128)} copy(s32[16,4]{0,1:T(4,128)} %param.10) | data formatting | bytes 512 | tf_op args[2]
  2.0 1.4 %copy.12.wts_ref = f32[16,4]{1,0:T(8,128)} copy(f32[16,4]{0,1:T(4,128)} %param.11) | data formatting | bytes 512 | tf_op args[3]
  3.3 59.0 %shard_map.103 = (bf16[16,3072]{1,0:T(8,128)(2,1)}, bf16[16,3072]{1,0:T(8,128)(2,1)}, f32[16,4]{1,0:T(8,128)}) custom-call(bf16[16,3072]{1,0:T(8,128)(2,1)} %q_ref.1, s32[16,24]{1,0:T(8,128)} %exp_ref.1, s32[16,4]{1,0:T(8,128)} %copy.11.ids_ref, f32[16,4]{1,0:T(8,128)} %copy.12.wts_ref, bf16[16,3072]{1,0:T(8,128)(2,1)} %cot_ref.1, ...), custom_call_target="tpu_custom_call" | custom-call | flops 12683575296 | bytes 49545216 | tf_op jit(solution)/shard_map/pallas_call | solution.py:297
  62.4 1.3 %copy.13 = f32[16,4]{0,1:T(4,128)} copy(f32[16,4]{1,0:T(8,128)} %get-tuple-element.5) | data formatting | bytes 512 | tf_op jit(solution)/shard_map/pallas_call | solution.py:297
  63.7 1.5 %copy.16 = bf16[16,3072]{1,0:T(8,128)(2,1)} copy(bf16[16,3072]{1,0:T(8,128)(2,1)} %get-tuple-element.9) | data formatting | bytes 196608
  65.3 1.5 %copy.17 = bf16[16,3072]{1,0:T(8,128)(2,1)} copy(bf16[16,3072]{1,0:T(8,128)(2,1)} %get-tuple-element.10) | data formatting | bytes 196608

commit v3 on v2

--- a/solution.py
+++ b/solution.py
@@ -29,8 +29,7 @@
     gate_hbm,
     up_hbm,
     down_hbm,
-    mixed_ref,
-    gtok_ref,
+    rows_ref,
     gwts_ref,
     xg,
     ret,
@@ -122,16 +121,21 @@
         for copy in weight_copies(c):
             copy.start()
 
-    toks, picks = ids_ref.shape
-    ids = ids_ref[...]
-    wts = wts_ref[...]
+    picks, toks = ids_ref.shape
+    later = lax.broadcasted_iota(jnp.int32, (toks, toks), 0)
+    earlier = lax.broadcasted_iota(jnp.int32, (toks, toks), 1)
+
+    def column(row):
+        return jnp.sum(jnp.where(later == earlier, row, 0.0), axis=1, keepdims=True)
+
+    ids = [column(ids_ref[k : k + 1, :].astype(jnp.float32)) for k in range(picks)]
+    wts = [column(wts_ref[k : k + 1, :]) for k in range(picks)]
     place = lax.broadcasted_iota(jnp.int32, (toks, half), 1)
-    hits = [(ids[:, k : k + 1] == place // CAP).astype(jnp.float32) for k in range(picks)]
+    expert_of = (place // CAP).astype(jnp.float32)
+    hits = [(ids[k] == expert_of).astype(jnp.float32) for k in range(picks)]
     named = hits[0]
     for k in range(1, picks):
         named = named + hits[k]
-    later = lax.broadcasted_iota(jnp.int32, (toks, toks), 0)
-    earlier = lax.broadcasted_iota(jnp.int32, (toks, toks), 1)
     below = (earlier < later).astype(jnp.bfloat16)
     before = jnp.dot(below, named.astype(jnp.bfloat16), preferred_element_type=jnp.float32)
     in_slot = (before == (place % CAP).astype(jnp.float32)).astype(jnp.float32)
@@ -149,7 +153,7 @@
             parts.append((part * scales[:, b : b + 1]).astype(jnp.bfloat16))
         toks_c = jnp.concatenate(parts, axis=1)
         grad32 = cot_ref[:, pl.ds(c * dc, dc)].astype(jnp.float32)
-        scaled = jnp.concatenate([wts[:, k : k + 1] * grad32 for k in range(picks)], axis=0)
+        scaled = jnp.concatenate([wts[k] * grad32 for k in range(picks)], axis=0)
         xs = lax.dot_general(placer_tok, toks_c, TN, preferred_element_type=jnp.float32)
         gs = lax.dot_general(
             placer, scaled.astype(jnp.bfloat16), TN, preferred_element_type=jnp.float32
@@ -197,16 +201,17 @@
             acc[0, :, cols] += gate
             acc[1, :, cols] += up
             acc[2, :, cols] += back
+            if f == 0:
+
+                @pl.when(c + 1 < chunks)
+                def _():
+                    collect(c + 1)
 
     acc[...] = jnp.zeros_like(acc)
     collect(0)
 
     @pl.loop(0, chunks)
     def _(c):
-        @pl.when(c + 1 < chunks)
-        def _():
-            collect(c + 1)
-
         project(c)
 
     e_tile = ff // E_TILES
@@ -250,12 +255,11 @@
             own[c % 2, :, CAP:, cols] = dx[0]
             pair_out[c % 2, :, :CAP, cols] = y[1]
             pair_out[c % 2, :, CAP:, cols] = dx[1]
+            if c >= 1 and d == 0:
+                finish(c - 1)
         pair(c).start()
-        if c >= 1:
-            finish(c - 1)
     finish(chunks - 1)
 
-    lane = lax.broadcasted_iota(jnp.int32, (toks, picks), 1)
     gwts_ref[...] = jnp.zeros_like(gwts_ref)
 
     @pl.loop(0, chunks)
@@ -270,16 +274,15 @@
         picked = jnp.dot(placer, ys, preferred_element_type=jnp.float32)
         grad32 = cot_ref[:, cols].astype(jnp.float32)
         total = jnp.zeros((toks, dc), jnp.float32)
-        dots = jnp.zeros((toks, picks), jnp.float32)
+        dots = []
         for k in range(picks):
             pick = picked[k * toks : (k + 1) * toks]
-            total = total + wts[:, k : k + 1] * pick
-            dots = jnp.where(lane == k, jnp.sum(grad32 * pick, axis=1, keepdims=True), dots)
-        gwts_ref[...] += dots
-        mixed_ref[:, cols] = total.astype(jnp.bfloat16)
-        gtok_ref[:, cols] = jnp.dot(
-            placer_tok, dxs, preferred_element_type=jnp.float32
-        ).astype(jnp.bfloat16)
+            total = total + wts[k] * pick
+            dot = jnp.sum(grad32 * pick, axis=1, keepdims=True)
+            dots.append(jnp.sum(jnp.where(later == earlier, dot, 0.0), axis=0, keepdims=True))
+        gwts_ref[...] += jnp.concatenate(dots, axis=0)
+        rows_ref[0, :, cols] = total
+        rows_ref[1, :, cols] = jnp.dot(placer_tok, dxs, preferred_element_type=jnp.float32)
 
     for c in range(chunks):
         forward(c).wait_send()
@@ -292,18 +295,17 @@
 def fused_experts(experts, rows_in, exps, ids, wts, cot, gate_w, up_w, down_w):
     toks, width = rows_in.shape
     ff = gate_w.shape[1]
-    c, dc, rows = CHUNKS, width // CHUNKS, 2 * experts * CAP
+    c, dc, slots = CHUNKS, width // CHUNKS, 2 * experts * CAP
     dma = pltpu.SemaphoreType.DMA
-    return pl.pallas_call(
+    rows, gwts = pl.pallas_call(
         functools.partial(fused_kernel, experts),
         out_shape=(
-            jax.ShapeDtypeStruct((toks, width), jnp.bfloat16),
-            jax.ShapeDtypeStruct((toks, width), jnp.bfloat16),
+            jax.ShapeDtypeStruct((2, toks, width), jnp.float32),
             jax.ShapeDtypeStruct(ids.shape, jnp.float32),
         ),
         in_specs=[pl.BlockSpec(memory_space=pltpu.VMEM)] * 5
         + [pl.BlockSpec(memory_space=pl.ANY)] * 3,
-        out_specs=[pl.BlockSpec(memory_space=pltpu.VMEM)] * 3,
+        out_specs=[pl.BlockSpec(memory_space=pltpu.VMEM)] * 2,
         scratch_shapes=[
             pltpu.VMEM((c, experts, 2 * CAP, dc), jnp.bfloat16),
             pltpu.VMEM((c, experts, 2 * CAP, dc), jnp.bfloat16),
@@ -311,8 +313,8 @@
             pltpu.VMEM((c, dc, ff), jnp.bfloat16),
             pltpu.VMEM((c, ff, dc), jnp.bfloat16),
             pltpu.VMEM((c, 2, experts, 2 * CAP, dc), jnp.bfloat16),
-            pltpu.VMEM((3, rows, ff), jnp.float32),
-            pltpu.VMEM((3, rows, ff), jnp.bfloat16),
+            pltpu.VMEM((3, slots, ff), jnp.float32),
+            pltpu.VMEM((3, slots, ff), jnp.bfloat16),
             pltpu.VMEM((2, experts, 2 * CAP, dc), jnp.float32),
             pltpu.VMEM((2, experts, 2 * CAP, dc), jnp.float32),
             pltpu.VMEM((c, experts, 2 * CAP, dc), jnp.float32),
@@ -330,9 +332,10 @@
             collective_id=0, has_side_effects=True, vmem_limit_bytes=63 * 2**20
         ),
         cost_estimate=pl.CostEstimate(
-            flops=12 * rows * width * ff, bytes_accessed=6 * width * ff, transcendentals=rows * ff
+            flops=12 * slots * width * ff, bytes_accessed=6 * width * ff, transcendentals=slots * ff
         ),
     )(rows_in, exps, ids, wts, cot, gate_w, up_w, down_w)
+    return (rows[0].astype(jnp.bfloat16), rows[1].astype(jnp.bfloat16), gwts.T)
 
 
 def expert_pass(rows, grads, gate_w, up_w, down_w):
@@ -419,8 +422,8 @@
             experts,
             quant_rows,
             block_exps,
-            expert_ids,
-            route_weights,
+            expert_ids.T,
+            route_weights.T,
             cotangent,
             gate_weight[0],
             up_weight[0],

time: 67.1 us -> 69.7 us (1.039)
  Pallas kernels: 59 us -> 65.9 us
  local copies, waits for them, and re-layouts: 7.14 us -> 1.95 us
  other arithmetic: 0 us -> 1.02 us
    pallas_call x1, Pallas kernels: 59 us -> 65.9 us  [fused_experts(): pl.pallas_call(functools.partial(fused_kernel, experts), out_shape=(jax.S...]
    unnamed x4 -> x1, local copies, waits for them, and re-layouts: 5.79 us -> 1.26 us
    pallas_call x1 -> x0, local copies, waits for them, and re-layouts: 1.35 us -> none  [fused_experts(): pl.pallas_call(functools.partial(fused_kernel, experts), out_shape=(jax.S...]
    another operation x0 -> x1, other arithmetic: none -> 1.02 us
where the time goes in v3:
time: 69.7 us; the launch traced here: 69.5 us
  Pallas kernels  65.9 us (95%)
  local copies, waits for them, and re-layouts  1.95 us (3%)
  other arithmetic  1.02 us (1%)
    pallas_call x1, Pallas kernels, fused_experts(): pl.pallas_call(functools.partial(fused_kernel, experts), out_shape=(jax.S...  65.9 us

profile of v3, /device:TPU:0, one launch (start us, length us, event | category | flops | bytes accessed | tf_op | source)
XLA Modules:
  0.0 69.5 jit_solution(9956571013930421150)
XLA Ops:
  0.6 65.9 %shard_map.103 = (f32[2,16,3072]{2,1,0:T(8,128)}, f32[4,16]{1,0:T(4,128)}) custom-call(bf16[16,3072]{1,0:T(8,128)(2,1)} %q_ref.1, s32[16,24]{1,0:T(8,128)} %exp_ref.1, s32[4,16]{1,0:T(4,128)} %bitcast.13, f32[4,16]{1,0:T(4,128)} %bitcast.14, bf16[16,3072]{1,0:T(8,128)(2,1)} %cot_ref.1, bf16[3072,2688]{1,0:T(8,128)(2,1)} %bitcast.10, ...), custom_call_target="tpu_custom_call" | custom-call | flops 12683575296 | bytes 49545216 | tf_op jit(solution)/shard_map/pallas_call | solution.py:300
  66.5 1.0 %convert.4 = bf16[2,16,3072]{2,1,0:T(8,128)(2,1)S(1)} convert(f32[2,16,3072]{2,1,0:T(8,128)} %get-tuple-element.5) | non-fusion elementwise | flops 98304 | bytes 589824 | tf_op jit(solution)/shard_map/convert.1
  67.5 0.7 slice_bitcast_fusion
  68.2 1.3 %copy.12 = f32[16,4]{0,1:T(4,128)} copy(f32[16,4]{0,1:T(4,128)} %bitcast.15) | data formatting | bytes 512

commit v4 on v3

--- a/solution.py
+++ b/solution.py
@@ -201,17 +201,16 @@
             acc[0, :, cols] += gate
             acc[1, :, cols] += up
             acc[2, :, cols] += back
-            if f == 0:
-
-                @pl.when(c + 1 < chunks)
-                def _():
-                    collect(c + 1)
 
     acc[...] = jnp.zeros_like(acc)
     collect(0)
 
     @pl.loop(0, chunks)
     def _(c):
+        @pl.when(c + 1 < chunks)
+        def _():
+            collect(c + 1)
+
         project(c)
 
     e_tile = ff // E_TILES
@@ -255,9 +254,9 @@
             own[c % 2, :, CAP:, cols] = dx[0]
             pair_out[c % 2, :, :CAP, cols] = y[1]
             pair_out[c % 2, :, CAP:, cols] = dx[1]
-            if c >= 1 and d == 0:
-                finish(c - 1)
         pair(c).start()
+        if c >= 1:
+            finish(c - 1)
     finish(chunks - 1)
 
     gwts_ref[...] = jnp.zeros_like(gwts_ref)

time: 69.7 us -> 63 us (0.904)
  Pallas kernels: 65.9 us -> 59.2 us
    pallas_call x1, Pallas kernels: 65.9 us -> 59.2 us  [fused_experts(): pl.pallas_call(functools.partial(fused_kernel, experts), out_shape=(jax.S...]
where the time goes in v4:
time: 63 us; the launch traced here: 62.8 us
  Pallas kernels  59.2 us (94%)
  local copies, waits for them, and re-layouts  1.95 us (3%)
  other arithmetic  1.02 us (2%)
  between operations  0.64 us (1%)
    pallas_call x1, Pallas kernels, fused_experts(): pl.pallas_call(functools.partial(fused_kernel, experts), out_shape=(jax.S...  59.2 us

profile of v4, /device:TPU:0, one launch (start us, length us, event | category | flops | bytes accessed | tf_op | source)
XLA Modules:
  0.0 62.8 jit_solution(16334964675918067553)
XLA Ops:
  0.6 59.2 %shard_map.103 = (f32[2,16,3072]{2,1,0:T(8,128)}, f32[4,16]{1,0:T(4,128)}) custom-call(bf16[16,3072]{1,0:T(8,128)(2,1)} %q_ref.1, s32[16,24]{1,0:T(8,128)} %exp_ref.1, s32[4,16]{1,0:T(4,128)} %bitcast.13, f32[4,16]{1,0:T(4,128)} %bitcast.14, bf16[16,3072]{1,0:T(8,128)(2,1)} %cot_ref.1, bf16[3072,2688]{1,0:T(8,128)(2,1)} %bitcast.10, ...), custom_call_target="tpu_custom_call" | custom-call | flops 12683575296 | bytes 49545216 | tf_op jit(solution)/shard_map/pallas_call | solution.py:299
  59.8 1.0 %convert.4 = bf16[2,16,3072]{2,1,0:T(8,128)(2,1)S(1)} convert(f32[2,16,3072]{2,1,0:T(8,128)} %get-tuple-element.5) | non-fusion elementwise | flops 98304 | bytes 589824 | tf_op jit(solution)/shard_map/convert.1
  60.8 0.7 %slice_bitcast_fusion = (bf16[16,3072]{1,0:T(8,128)(2,1)}, bf16[16,3072]{1,0:T(8,128)(2,1)}) fusion(bf16[2,16,3072]{2,1,0:T(8,128)(2,1)S(1)} %convert.4), kind=kLoop, calls=%fused_computation | loop fusion | bytes 393216 | tf_op jit(solution)/shard_map/convert_element_type | solution.py:337
  61.5 1.3 %copy.12 = f32[16,4]{0,1:T(4,128)} copy(f32[16,4]{0,1:T(4,128)} %bitcast.15) | data formatting | bytes 512
